TPU v7x, 256 devices: a whole 4x4x8 slice. The times are simulated.
256 devices in a mesh: dp: 8 (over x, core), head: 32 (over z, y).
Axes of the slice: x: 4, y: 4, z: 8, core: 2. Of those that a mesh axis runs over, the one named last changes fastest.
Arguments:
- query_latent: bfloat16 [4, 256, 1536], P(None, ('dp', 'head')), may hold values from -6 to 6
- query_weight: bfloat16 [1536, 24576], P(('dp', 'head')), may hold values from -0.15625 to 0.15625
- key_weight: bfloat16 [512, 16384], P(('dp', 'head')), may hold values from -0.25 to 0.25
- value_weight: bfloat16 [512, 16384], P(('dp', 'head')), may hold values from -0.25 to 0.25
- cache_latent: bfloat16 [256, 2048, 512], P(('dp', 'head')), may hold values from -6 to 6
- cache_rope: bfloat16 [256, 64, 2048], P(('dp', 'head')), may hold values from -1000 to 1000
- new_latent: bfloat16 [4, 256, 512], P(None, ('dp', 'head')), may hold values from -6 to 6
- new_rope: bfloat16 [4, 256, 64], P(None, ('dp', 'head')), may hold values from -6 to 6
- lengths: int32 [256], P(('dp', 'head')), may hold values from 1 to 2048, as said below
Outputs:
- attended: bfloat16 [4, 256, 16384], P(None, 'dp', 'head')
Inputs may be any that keep to these rules, and one draw needn't show every extreme that they name: `lengths`: each sequence has at least one filled slot; some sequence fills all 2048.
All inputs are finite; a program needn't handle non-finite values.
Results may differ from a plain program's by a relative error of at most 0.014.
Values may be sent and summed in bfloat16 or wider, within the bound.
A program may use at most 128 MiB of HBM per device.

v0:
```python
import jax
import jax.numpy as jnp
from jax import lax
from jax.sharding import PartitionSpec as P

QR = 1536
KVR = 512
DN = 128
DR = 64
DV = 128


def attend(query_abs, query_pos, latent, rope, fresh_latent, fresh_rope, length):
    steps_here = query_abs.shape[0]
    heads = query_abs.shape[1]
    scale = (DN + DR) ** (-0.5)
    query_rows = query_abs.reshape(steps_here * heads, KVR)
    pos_rows = query_pos.reshape(steps_here * heads, DR)
    cached = (
        jnp.dot(query_rows, latent.T, preferred_element_type=jnp.float32)
        + jnp.dot(pos_rows, rope, preferred_element_type=jnp.float32)
    ) * scale
    fresh = (
        jnp.dot(query_rows, fresh_latent.T, preferred_element_type=jnp.float32)
        + jnp.dot(pos_rows, fresh_rope.T, preferred_element_type=jnp.float32)
    ) * scale
    slots = jnp.arange(latent.shape[0], dtype=jnp.int32)
    cached = jnp.where(slots[None, :] < length, cached, jnp.float32(-1e30))
    row_step = jnp.arange(steps_here * heads, dtype=jnp.int32) // heads
    later = jnp.arange(steps_here, dtype=jnp.int32)
    fresh = jnp.where(later[None, :] <= row_step[:, None], fresh, jnp.float32(-1e30))
    top = jnp.maximum(jnp.max(cached, axis=1, keepdims=True), jnp.max(fresh, axis=1, keepdims=True))
    exp_cached = jnp.exp(cached - top)
    exp_fresh = jnp.exp(fresh - top)
    total = jnp.sum(exp_cached, axis=1, keepdims=True) + jnp.sum(exp_fresh, axis=1, keepdims=True)
    probs_cached = (exp_cached / total).astype(jnp.bfloat16)
    probs_fresh = (exp_fresh / total).astype(jnp.bfloat16)
    mixed = jnp.dot(probs_cached, latent, preferred_element_type=jnp.float32) + jnp.dot(
        probs_fresh, fresh_latent, preferred_element_type=jnp.float32
    )
    return mixed.astype(jnp.bfloat16).reshape(steps_here, heads, KVR)


def regroup(arranged, outer, inner):
    columns = arranged.shape[1]
    shard_rows = arranged.shape[0] // (outer * inner)
    arranged = arranged.reshape(outer, inner, shard_rows, columns)
    return jnp.swapaxes(arranged, 0, 1).reshape(outer * inner * shard_rows, columns)


def body(
    query_latent,
    query_weight,
    key_weight,
    value_weight,
    cache_latent,
    cache_rope,
    new_latent,
    new_rope,
    lengths,
):
    rows_query, rows_key, rows_value = (
        lax.all_gather(query_weight, "dp", axis=0, tiled=True),
        lax.all_gather(key_weight, "dp", axis=0, tiled=True),
        lax.all_gather(value_weight, "dp", axis=0, tiled=True),
    )
    owned_query, owned_key, owned_value = (
        lax.all_to_all(rows_query, "head", split_axis=1, concat_axis=0, tiled=True),
        lax.all_to_all(rows_key, "head", split_axis=1, concat_axis=0, tiled=True),
        lax.all_to_all(rows_value, "head", split_axis=1, concat_axis=0, tiled=True),
    )
    replicas = lax.axis_size("dp")
    owners = lax.axis_size("head")
    full_query = regroup(owned_query, owners, replicas)
    full_key = regroup(owned_key, owners, replicas)
    full_value = regroup(owned_value, owners, replicas)
    local_heads = full_key.shape[1] // DN
    weight_heads = full_query.reshape(QR, local_heads, DN + DR)
    key_heads = full_key.reshape(KVR, local_heads, DN)
    absorbed = jnp.einsum(
        "chd,khd->chk", weight_heads[:, :, :DN], key_heads, preferred_element_type=jnp.float32
    ).astype(jnp.bfloat16)
    absorbed = absorbed.reshape(QR, local_heads * KVR)
    pos_weight = weight_heads[:, :, DN:].reshape(QR, local_heads * DR)
    replica_queries = lax.all_gather(query_latent, "head", axis=1, tiled=True)
    steps_here = replica_queries.shape[0]
    replica_seqs = replica_queries.shape[1]
    query_rows = replica_queries.reshape(steps_here * replica_seqs, QR)
    query_abs = jnp.dot(query_rows, absorbed, preferred_element_type=jnp.float32).astype(
        jnp.bfloat16
    )
    query_abs = query_abs.reshape(steps_here, replica_seqs, local_heads * KVR)
    query_pos = jnp.dot(query_rows, pos_weight, preferred_element_type=jnp.float32).astype(
        jnp.bfloat16
    )
    query_pos = query_pos.reshape(steps_here, replica_seqs, local_heads * DR)
    own_abs, own_pos = (
        lax.all_to_all(query_abs, "head", split_axis=1, concat_axis=2, tiled=True),
        lax.all_to_all(query_pos, "head", split_axis=1, concat_axis=2, tiled=True),
    )
    own_seqs = own_abs.shape[1]
    all_heads = own_abs.shape[2] // KVR
    own_abs = jnp.swapaxes(own_abs.reshape(steps_here, own_seqs, all_heads, KVR), 0, 1)
    own_pos = jnp.swapaxes(own_pos.reshape(steps_here, own_seqs, all_heads, DR), 0, 1)

    def one_sequence(items):
        return attend(*items)

    latent_out = lax.map(
        one_sequence,
        (
            own_abs,
            own_pos,
            cache_latent,
            cache_rope,
            jnp.swapaxes(new_latent, 0, 1),
            jnp.swapaxes(new_rope, 0, 1),
            lengths,
        ),
    )
    latent_out = jnp.swapaxes(latent_out, 0, 1).reshape(steps_here, own_seqs, all_heads * KVR)
    head_latent = lax.all_to_all(latent_out, "head", split_axis=2, concat_axis=1, tiled=True)
    head_latent = head_latent.reshape(steps_here, replica_seqs, local_heads, KVR)
    value_heads = full_value.reshape(KVR, local_heads, DV)
    attended = jnp.einsum(
        "sbhk,khv->sbhv", head_latent, value_heads, preferred_element_type=jnp.float32
    )
    return attended.astype(jnp.bfloat16).reshape(steps_here, replica_seqs, local_heads * DV)


def solution(mesh):
    placed = (
        P(None, ("dp", "head"), None),
        P(("dp", "head"), None),
        P(("dp", "head"), None),
        P(("dp", "head"), None),
        P(("dp", "head"), None, None),
        P(("dp", "head"), None, None),
        P(None, ("dp", "head"), None),
        P(None, ("dp", "head"), None),
        P(("dp", "head")),
    )
    return jax.shard_map(
        body, mesh=mesh, in_specs=placed, out_specs=P(None, "dp", "head"), check_vma=False
    )
```

profile of v0, /device:TPU:1, one launch (start us, length us, event | category | flops | bytes accessed | tf_op | source)
XLA Modules:
  0.0 830.0 jit_solution(3718189191474421185)
XLA Ops:
  7.3 16.4 %all-gather = bf16[8,2,16384]{2,1,0:T(2,128)(2,1)S(1)} all-gather(bf16[1,2,16384]{2,1,0:T(2,128)(2,1)} %bitcast.81), channel_id=1, replica_groups=mesh['dp'=8,'head'=32] {'dp'}, dimensions={0}, use_global_device_ids=true | all-gather | bytes 589824 | tf_op jit(solution)/shard_map/all_gather | solution.py:64
  25.1 9.8 %all-to-all-start = ((bf16[16,32,512]{2,0,1:T(8,128)(2,1)}), bf16[16,32,512]{2,0,1:T(8,128)(2,1)S(1)}, u32[]{:S(2)}, u32[]{:S(2)}) async-start(bf16[16,32,512]{2,0,1:T(8,128)(2,1)} %copy.48), calls=%async_computation | async-start | bytes 1048576 | tf_op jit(solution)/shard_map/all_to_all | solution.py:69
  34.9 8.8 %all-gather.5.cloned.1.call-done = bf16[8,6,24576]{2,1,0:T(8,128)(2,1)} async-done(((bf16[1,6,24576]{2,1,0:T(8,128)(2,1)}), bf16[8,6,24576]{2,1,0:T(8,128)(2,1)}) %all-gather.5.cloned.1.call-update) | async-done | bytes 2359312 | tf_op jit(solution)/shard_map/all_gather | solution.py:63
  43.7 6.1 all_to_all.60
  49.8 4.4 copy.51
  54.2 9.7 %all-to-all-start.1 = ((bf16[48,32,768]{2,0,1:T(8,128)(2,1)}), bf16[48,32,768]{2,0,1:T(8,128)(2,1)}, u32[]{:S(2)}, u32[]{:S(2)}) async-start(bf16[48,32,768]{2,0,1:T(8,128)(2,1)} %copy.51), calls=%async_computation.1 | async-start | bytes 4718592 | tf_op jit(solution)/shard_map/all_to_all | solution.py:68
  63.9 84.6 %all_gather.14 = bf16[4,32,1536]{2,0,1:T(4,128)(2,1)S(1)} all-gather(bf16[4,1,1536]{2,0,1:T(4,128)(2,1)S(1)} %copy-done.7), channel_id=1, replica_groups=mesh['dp'=8,'head'=32] {'head'}, dimensions={1}, use_global_device_ids=true | all-gather | bytes 405504 | tf_op jit(solution)/shard_map/all_gather | solution.py:85
  150.5 2.4 copy.52
  152.9 3.2 copy.53
  156.1 7.8 reshape_reshape.10
  163.9 2.7 slice.8
  168.1 2.6 copy.59
  172.8 15.9 %all-to-all-start.3 = ((bf16[4,32,256]{2,0,1:T(4,128)(2,1)}), bf16[4,32,256]{2,0,1:T(4,128)(2,1)S(1)}, u32[]{:S(2)}, u32[]{:S(2)}) async-start(bf16[4,32,256]{2,0,1:T(4,128)(2,1)} %copy.60), calls=%async_computation.3 | async-start | bytes 131072 | tf_op jit(solution)/shard_map/all_to_all | solution.py:99
  188.7 3.3 convolution_convert_fusion
  197.5 7.1 all-to-all-start.2
  205.3 27.5 %all-gather.2 = bf16[8,2,16384]{2,1,0:T(2,128)(2,1)} all-gather(bf16[1,2,16384]{2,1,0:T(2,128)(2,1)S(1)} %bitcast.82), channel_id=1, replica_groups=mesh['dp'=8,'head'=32] {'dp'}, dimensions={0}, use_global_device_ids=true | all-gather | bytes 589824 | tf_op jit(solution)/shard_map/all_gather | solution.py:65
  235.4 9.5 %all-to-all-start.5 = ((bf16[16,32,512]{2,0,1:T(8,128)(2,1)}), bf16[16,32,512]{2,0,1:T(8,128)(2,1)S(1)}, u32[]{:S(2)}, u32[]{:S(2)}) async-start(bf16[16,32,512]{2,0,1:T(8,128)(2,1)} %copy.64), calls=%async_computation.5 | async-start | bytes 1048576 | tf_op jit(solution)/shard_map/all_to_all | solution.py:70
  252.9 50.4 %copy.62 = bf16[4,1,65536]{0,1,2:T(2,128)(2,1)} copy(bf16[4,1,65536]{2,0,1:T(4,128)(2,1)S(1)} %reshape_transpose.3) | data formatting | bytes 1048576 | tf_op jit(solution)/shard_map/reshape;transpose | solution.py:121
  303.9 356.0 %reduce = bf16[65536,4]{1,0:T(8,128)(2,1)} reduce(bf16[65536,1,4]{2,1,0:T(2,128)(2,1)} %bitcast.68, bf16[]{:T(256)} %broadcast.50), dimensions={1}, to_apply=%bitcast.52.reduce_sub_computation | reduce | bytes 1048578
  659.9 31.8 %reshape.124 = bf16[32,2,4096]{2,1,0:T(2,128)(2,1)} reshape(bf16[65536,4]{1,0:T(8,128)(2,1)} %reduce) | data formatting | bytes 1048576
  691.7 9.2 %all-to-all-start.4 = ((bf16[32,2,4096]{2,1,0:T(2,128)(2,1)}), bf16[32,2,4096]{2,1,0:T(2,128)(2,1)S(1)}, u32[]{:S(2)}, u32[]{:S(2)}) async-start(bf16[32,2,4096]{2,1,0:T(2,128)(2,1)} %reshape.124), calls=%async_computation.4 | async-start | bytes 1048576 | tf_op jit(solution)/shard_map/all_to_all | solution.py:122
  702.1 14.9 %all-to-all-done.4 = bf16[32,2,4096]{2,1,0:T(2,128)(2,1)S(1)} async-done(((bf16[32,2,4096]{2,1,0:T(2,128)(2,1)}), bf16[32,2,4096]{2,1,0:T(2,128)(2,1)S(1)}, u32[]{:S(2)}, u32[]{:S(2)}) %all-to-all-start.4) | async-done | bytes 524320 | tf_op jit(solution)/shard_map/all_to_all | solution.py:122
  717.0 41.5 %reshape.125 = bf16[65536,1,4]{2,1,0:T(2,128)(2,1)} reshape(bf16[32,2,4096]{2,1,0:T(2,128)(2,1)S(1)} %all-to-all-done.4) | data formatting | bytes 1048576
  758.5 61.1 %copy.63 = bf16[4,1,65536]{2,0,1:T(4,128)(2,1)S(1)} copy(bf16[4,1,65536]{0,1,2:T(2,128)(2,1)} %bitcast.69) | data formatting | bytes 1048576 | tf_op jit(solution)/shard_map/all_to_all | solution.py:122
  (62 shorter events, 28.8 us)
Async XLA Ops:
  6.5 241.1 %copy-start = (bf16[1,2048,512]{2,1,0:T(8,128)(2,1)S(1)}, bf16[1,2048,512]{2,1,0:T(8,128)(2,1)}, u32[]{:S(2)}) copy-start(bf16[1,2048,512]{2,1,0:T(8,128)(2,1)} %param.13) | copy-start | bytes 6291460
  6.5 37.2 %all-gather.5.cloned.1.call-start = ((), (), s32[]{:S(2)}) async-start(), calls=%async_computation.6 | async-start | bytes 3538944 | tf_op jit(solution)/shard_map/all_gather | solution.py:63
  25.1 29.0 %all-to-all-start = ((bf16[16,32,512]{2,0,1:T(8,128)(2,1)}), bf16[16,32,512]{2,0,1:T(8,128)(2,1)S(1)}, u32[]{:S(2)}, u32[]{:S(2)}) async-start(bf16[16,32,512]{2,0,1:T(8,128)(2,1)} %copy.48), calls=%async_computation | async-start | bytes 1048576 | tf_op jit(solution)/shard_map/all_to_all | solution.py:69
  49.8 14.1 %copy-start.7 = (bf16[4,1,1536]{2,0,1:T(4,128)(2,1)S(1)}, bf16[4,1,1536]{2,0,1:T(4,128)(2,1)}, u32[]{:S(2)}) copy-start(bf16[4,1,1536]{2,0,1:T(4,128)(2,1)} %param.9) | copy-start | bytes 36868
  54.2 96.4 %all-to-all-start.1 = ((bf16[48,32,768]{2,0,1:T(8,128)(2,1)}), bf16[48,32,768]{2,0,1:T(8,128)(2,1)}, u32[]{:S(2)}, u32[]{:S(2)}) async-start(bf16[48,32,768]{2,0,1:T(8,128)(2,1)} %copy.51), calls=%async_computation.1 | async-start | bytes 4718592 | tf_op jit(solution)/shard_map/all_to_all | solution.py:68
  163.9 2.7 copy-start.2
  172.8 24.8 %all-to-all-start.3 = ((bf16[4,32,256]{2,0,1:T(4,128)(2,1)}), bf16[4,32,256]{2,0,1:T(4,128)(2,1)S(1)}, u32[]{:S(2)}, u32[]{:S(2)}) async-start(bf16[4,32,256]{2,0,1:T(4,128)(2,1)} %copy.60), calls=%async_computation.3 | async-start | bytes 131072 | tf_op jit(solution)/shard_map/all_to_all | solution.py:99
  188.7 3.3 copy-start.3
  192.0 13.2 %copy-start.5 = (bf16[2,16384]{1,0:T(2,128)(2,1)S(1)}, bf16[2,16384]{1,0:T(2,128)(2,1)}, u32[]{:S(2)}) copy-start(bf16[2,16384]{1,0:T(2,128)(2,1)} %param.12) | copy-start | bytes 196612
  194.2 53.2 %copy-start.6 = (bf16[4,1,512]{2,0,1:T(4,128)(2,1)S(1)}, bf16[4,1,512]{2,0,1:T(4,128)(2,1)}, u32[]{:S(2)}) copy-start(bf16[4,1,512]{2,0,1:T(4,128)(2,1)} %param.15) | copy-start | bytes 12292
  197.5 37.8 %all-to-all-start.2 = ((bf16[4,32,2048]{2,0,1:T(4,128)(2,1)}), bf16[4,32,2048]{2,0,1:T(4,128)(2,1)S(1)}, u32[]{:S(2)}, u32[]{:S(2)}) async-start(bf16[4,32,2048]{2,0,1:T(4,128)(2,1)} %copy.57), calls=%async_computation.2 | async-start | bytes 1048576 | tf_op jit(solution)/shard_map/all_to_all | solution.py:98
  235.4 456.3 %all-to-all-start.5 = ((bf16[16,32,512]{2,0,1:T(8,128)(2,1)}), bf16[16,32,512]{2,0,1:T(8,128)(2,1)S(1)}, u32[]{:S(2)}, u32[]{:S(2)}) async-start(bf16[16,32,512]{2,0,1:T(8,128)(2,1)} %copy.64), calls=%async_computation.5 | async-start | bytes 1048576 | tf_op jit(solution)/shard_map/all_to_all | solution.py:70
  247.6 1.3 copy-start.8
  247.6 1.5 copy-start.4
  691.7 25.3 %all-to-all-start.4 = ((bf16[32,2,4096]{2,1,0:T(2,128)(2,1)}), bf16[32,2,4096]{2,1,0:T(2,128)(2,1)S(1)}, u32[]{:S(2)}, u32[]{:S(2)}) async-start(bf16[32,2,4096]{2,1,0:T(2,128)(2,1)} %reshape.124), calls=%async_computation.4 | async-start | bytes 1048576 | tf_op jit(solution)/shard_map/all_to_all | solution.py:122
  758.5 64.3 %copy-start.1 = (bf16[1,2048,512]{2,1,0:T(8,128)(2,1)S(1)}, bf16[1,2048,512]{2,1,0:T(8,128)(2,1)}, u32[]{:S(2)}) copy-start(bf16[1,2048,512]{2,1,0:T(8,128)(2,1)} %param.13) | copy-start | bytes 6291460
Sparse Core Ops, SparseCore 0:
  9.2 34.4 all-gather.4
where the time goes:
time: 841 us; the launch traced here: 830 us
  other arithmetic  357 us (42%)
  local copies, waits for them, and re-layouts  230 us (27%)
  blocking collectives  128 us (15%)
  starting transfers between devices  61.2 us (7%)
  waiting for transfers between devices  26.5 us (3%)
  between operations  14.7 us (2%)
  matrix products  12.5 us (1%)
    unnamed x1, other arithmetic  356 us
    all_gather x1, blocking collectives, body(): replica_queries = lax.all_gather(query_latent, 'head', axis=1, tiled=True)  84.6 us
    unnamed x21, local copies, waits for them, and re-layouts  73.9 us
    all_to_all x1, local copies, waits for them, and re-layouts, body(): lax.all_to_all(latent_out, 'head', split_axis=2, concat_axis=1, tiled=True)  61.1 us
    another operation x2, local copies, waits for them, and re-layouts, body(): jnp.swapaxes(latent_out, 0, 1)  50.8 us
    all_gather x1, blocking collectives, body(): lax.all_gather(value_weight, 'dp', axis=0, tiled=True)  27.5 us
  transfers between devices with their start and end apart: 7, of which 3 were waited for; matrix products, arithmetic and copies ran while one was open for 56% of the time, Pallas kernels for 0%

commit v1 on v0

v1 whole, which is shorter than its diff:
```python
import functools
import math

import jax
import jax.numpy as jnp
from jax import lax
from jax.experimental import pallas as pl
from jax.experimental.pallas import tpu as pltpu
from jax.sharding import PartitionSpec as P

QR = 1536
KVR = 512
DN = 128
DR = 64
DV = 128
CACHE = 2048
STEPS = 4
GROUPS = 32
HEADS = 4
RINGX = 4
DP = 8
KEYS = CACHE + 128
WIDE = KVR + 128
ROWS = GROUPS * HEADS * STEPS
BLOCK = 8
NB = GROUPS // BLOCK
BF = jnp.bfloat16
F32 = jnp.float32
MESH = pl.DeviceIdType.MESH


def iota(shape, dim):
    return lax.broadcasted_iota(jnp.int32, shape, dim)


def one_hot(source, columns):
    rows = source.shape[0]
    return jnp.where(iota((rows, columns), 1) == source, 1.0, 0.0).astype(BF)


def mm(a, b):
    return jnp.dot(a, b, preferred_element_type=F32)


def mm_t(a, b):
    return lax.dot_general(a, b, (((1,), (1,)), ((), ())), preferred_element_type=F32)


def kernel(
    q_ref, wq_ref, kw_ref, vw_ref, lat_hbm, rope_hbm, nl_ref, nr_ref, len_ref, out_ref,
    w32, k32, v32, small, pack, packv, qsend, rw, rv, rq, qnat, wqf, kvf, xs, send, recv, latx, kt,
    outs, back, lt, att,
    load_sem, snd, q_sem, w_sem, v_sem, a_sem, o_sem, xsnd, xrcv, vsnd, vrcv,
):
    dp = lax.axis_index("dp")
    me = lax.axis_index("head")
    xpos = dp // 2
    core = dp % 2
    right = ((xpos + 1) % RINGX) * 2 + core
    left = ((xpos + RINGX - 1) % RINGX) * 2 + core
    across = ((xpos + 2) % RINGX) * 2 + core
    other = xpos * 2 + (1 - core)

    def here(t):
        return {"dp": dp, "head": t}

    def peer(i):
        return lax.rem(me + i, GROUPS)

    barrier = pltpu.get_barrier_semaphore()

    def greet(i, carry):
        pl.semaphore_signal(barrier, inc=1, device_id=here(peer(i)), device_id_type=MESH)
        return carry

    lax.fori_loop(1, GROUPS, greet, 0)
    for d in (left, right, other):
        pl.semaphore_signal(barrier, inc=1, device_id={"dp": d, "head": me}, device_id_type=MESH)

    load_lat = pltpu.make_async_copy(lat_hbm.at[0], latx.at[pl.ds(0, CACHE)], load_sem.at[0])
    load_rope = pltpu.make_async_copy(rope_hbm.at[0], kt.at[pl.ds(KVR, DR), pl.ds(0, CACHE)], load_sem.at[1])
    load_lat.start()
    load_rope.start()

    for j in range(QR // 128):
        small[4 * j : 4 * j + 4, :] = q_ref[:, 128 * j : 128 * j + 128].astype(F32)
    qsend[...] = small[...].astype(BF)
    w32[6:8, :] = jnp.zeros((2, w32.shape[1]), F32)
    w32[0:6, :] = wq_ref[...].astype(F32)
    k32[0:6, :] = jnp.zeros((6, k32.shape[1]), F32)
    k32[6:8, :] = kw_ref[...].astype(F32)
    for b in range(HEADS):
        v32[2 * b : 2 * b + 2, :] = vw_ref[...].astype(F32)

    def pack_weights(t, carry):
        wide = pl.multiple_of(t * 768, 128)
        narrow = pl.multiple_of(t * 512, 128)
        parts = []
        for b in range(6):
            part = w32[:, pl.ds(wide + b * 128, 128)]
            if b < 4:
                part = part + k32[:, pl.ds(narrow + b * 128, 128)]
            parts.append(part)
        pack[t] = jnp.concatenate(parts, axis=0).astype(BF)
        return carry

    lax.fori_loop(0, GROUPS, pack_weights, 0)

    def pack_values(t, carry):
        narrow = pl.multiple_of(t * 512, 128)
        row = iota((8, 128), 0) // 2
        value = jnp.zeros((8, 128), F32)
        for b in range(HEADS):
            value = jnp.where(row == b, v32[:, pl.ds(narrow + b * 128, 128)], value)
        packv[t] = jnp.concatenate([value, jnp.zeros((8, 128), F32)], axis=0).astype(BF)
        return carry

    lax.fori_loop(0, GROUPS, pack_values, 0)

    pl.semaphore_wait(barrier, GROUPS - 1 + 3)

    mine = me // BLOCK

    def q_copy(i):
        return pltpu.make_async_remote_copy(qsend, rq.at[me], snd.at[0], q_sem.at[mine], here(peer(i)), MESH)

    def w_copy(i):
        t = peer(i)
        return pltpu.make_async_remote_copy(pack.at[t], rw.at[me], snd.at[1], w_sem.at[mine], here(t), MESH)

    def v_copy(i):
        t = peer(i)
        return pltpu.make_async_remote_copy(packv.at[t], rv.at[me], snd.at[2], v_sem.at[mine], here(t), MESH)

    def start_qw(i, carry):
        q_copy(i).start()
        w_copy(i).start()
        return carry

    def start_v(i, carry):
        v_copy(i).start()
        return carry

    own_q = pltpu.make_async_copy(qsend, rq.at[me], q_sem.at[mine])
    own_w = pltpu.make_async_copy(pack.at[me], rw.at[me], w_sem.at[mine])
    own_v = pltpu.make_async_copy(packv.at[me], rv.at[me], v_sem.at[mine])
    own_q.start()
    own_w.start()
    own_v.start()
    lax.fori_loop(1, GROUPS, start_qw, 0)
    lax.fori_loop(1, GROUPS, start_v, 0)

    def await_block(ref, sem, g):
        block = ref.at[pl.ds(g * BLOCK, BLOCK)]
        pltpu.make_async_copy(block, block, sem.at[g]).wait()

    small[0:8, :] = jnp.zeros((8, 128), F32)
    small[0:4, 0:DR] = nr_ref[...].astype(F32)
    fresh_rope = jnp.concatenate([small[0:8, :], jnp.zeros((120, 128), F32)], axis=0)
    kt[KVR:, CACHE:] = fresh_rope.T.astype(BF)
    kt[KVR + DR :, :CACHE] = jnp.zeros((128 - DR, CACHE), BF)
    for b in range(KVR // 128):
        small[0:8, :] = jnp.zeros((8, 128), F32)
        small[0:4, :] = nl_ref[:, b * 128 : b * 128 + 128].astype(F32)
        fresh = jnp.concatenate([small[0:8, :], jnp.zeros((120, 128), F32)], axis=0)
        latx[CACHE:, b * 128 : b * 128 + 128] = fresh.astype(BF)
    load_lat.wait()
    load_rope.wait()

    def turn(i, carry):
        at = pl.multiple_of(i * 128, 128)
        kt[0:KVR, pl.ds(at, 128)] = latx[pl.ds(at, 128), :].T
        return carry

    lax.fori_loop(0, KEYS // 128, turn, 0)

    o = iota((384, 1), 0)
    inside = o % 32
    q_order = one_hot((inside // 4) * 48 + (o // 32) * 4 + inside % 4, 384)
    for g in range(NB):
        await_block(rq, q_sem, g)
    arrived = jnp.concatenate([rq[g * BLOCK : (g + 1) * BLOCK].reshape(384, 128) for g in range(NB)], axis=1)
    ordered = mm(q_order, arrived).astype(BF)
    for j in range(QR // 128):
        for g in range(NB):
            qnat[g * 32 : g * 32 + 32, j * 128 : j * 128 + 128] = ordered[j * 32 : j * 32 + 32, g * 128 : g * 128 + 128]

    u = o % 64
    sixth = (u * 43) >> 8
    from_query = sixth * 48 + (o // 64) * 8 + (u - sixth * 6)
    from_key = ((u - 48) // 2) * 48 + (o // 64) * 8 + 6 + (u % 2)
    w_order = one_hot(jnp.where(u < 48, from_query, from_key), 384)
    for g in range(NB):
        await_block(rw, w_sem, g)
    arrived = jnp.concatenate([rw[g * BLOCK : (g + 1) * BLOCK].reshape(384, 128) for g in range(NB)], axis=1)
    ordered = mm(w_order, arrived).astype(BF)
    for b in range(6):
        for g in range(NB):
            lanes = slice(g * 128, g * 128 + 128)
            wqf[dp, g * 48 : g * 48 + 48, b * 128 : b * 128 + 128] = ordered[b * 64 : b * 64 + 48, lanes]
            if b < 4:
                kvf[dp, g * 16 : g * 16 + 16, b * 128 : b * 128 + 128] = ordered[b * 64 + 48 : b * 64 + 64, lanes]

    def ring(pieces, ssem, rsem):
        count = len(pieces)

        def copy(k, p, owner, to, part=None):
            ref, first, rows = pieces[p]
            if part is not None:
                rows = rows // 2
                first = first + part * rows
            view = ref.at[owner, pl.ds(first, rows)]
            slot = k * count + p
            return pltpu.make_async_remote_copy(
                view, view, ssem.at[slot], rsem.at[slot], {"dp": to, "head": me}, MESH
            )

        every = range(count)

        def begin():
            for p in every:
                copy(0, p, dp, right, 0).start()
                copy(1, p, dp, left, 1).start()
            for p in every:
                copy(2, p, dp, right, 1).start()
                copy(3, p, dp, left, 0).start()
            for p in every:
                copy(4, p, dp, other).start()

        def forward():
            for p in every:
                copy(0, p, left, right, 0).wait_recv()
                copy(5, p, left, right, 0).start()
                copy(1, p, right, left, 1).wait_recv()
                copy(6, p, right, left, 1).start()

        def neighbours():
            for p in every:
                copy(2, p, left, right, 1).wait_recv()
                copy(7, p, left, other).start()
                copy(3, p, right, left, 0).wait_recv()
                copy(8, p, right, other).start()

        def far():
            for p in every:
                copy(5, p, across, right, 0).wait_recv()
                copy(6, p, across, left, 1).wait_recv()
                copy(9, p, across, other).start()

        def finish():
            sib = 1 - 2 * core
            for p in every:
                copy(4, p, dp + sib, other).wait_recv()
                copy(7, p, left + sib, other).wait_recv()
                copy(8, p, right + sib, other).wait_recv()
                copy(9, p, across + sib, other).wait_recv()
            for p in every:
                for k, part in ((0, 0), (1, 1), (2, 1), (3, 0), (4, None), (5, 0), (6, 1), (7, None), (8, None), (9, None)):
                    copy(k, p, dp, right, part).wait_send()

        return begin, forward, neighbours, far, finish

    for step in ring([(wqf, 0, 192), (kvf, 0, 64)], xsnd, xrcv):
        step()

    projected = mm(qnat[...], wqf[...].reshape(QR, 768))
    xs[:, KVR:] = jnp.zeros((ROWS, WIDE - KVR), BF)
    for h in range(HEADS):
        at = h * (DN + DR)
        plain = projected[:, at : at + DN].astype(BF)
        keys = kvf[:, 0:64, h * DN : (h + 1) * DN].reshape(KVR, DN)
        xs[h * 128 : h * 128 + 128, 0:KVR] = mm_t(plain, keys).astype(BF)
        xs[h * 128 : h * 128 + 128, KVR : KVR + DR] = projected[:, at + DN : at + DN + DR].astype(BF)

    o = iota((128, 1), 0)
    by_seq = one_hot(((o // 4) % 4) * 32 + (o // 16) * 4 + o % 4, 128)
    by_head = one_hot(((o // 4) % 8) * 16 + (o // 32) * 4 + o % 4, 128)
    by_step = one_hot((o % 32) * 4 + o // 32, 128)

    def send_queries(k, carry):
        g = lax.rem(mine + k, NB)
        stacked = jnp.concatenate(
            [xs[pl.ds(pl.multiple_of(h * 128 + g * 32, 32), 32), :] for h in range(HEADS)], axis=0
        )
        send[pl.ds(g * BLOCK, BLOCK)] = mm(by_seq, stacked).astype(BF).reshape(BLOCK, 16, WIDE)

        def one(j, c):
            t = g * BLOCK + j

            @pl.when(t != me)
            def _():
                pltpu.make_async_remote_copy(
                    send.at[t], recv.at[me], snd.at[3], a_sem.at[mine], here(t), MESH
                ).start()

            return c

        lax.fori_loop(0, BLOCK, one, 0)
        return carry

    lax.fori_loop(0, NB, send_queries, 0)
    own_a = pltpu.make_async_copy(send.at[me], recv.at[me], a_sem.at[mine])
    own_a.start()

    o = iota((64, 1), 0)
    v_order = one_hot(((o % 16) // 2) * 16 + (o // 16) * 2 + o % 2, 128)
    for g in range(NB):
        await_block(rv, v_sem, g)
    arrived = jnp.concatenate([rv[g * BLOCK : (g + 1) * BLOCK].reshape(128, 128) for g in range(NB)], axis=1)
    ordered = mm(v_order, arrived).astype(BF)
    for b in range(4):
        for g in range(NB):
            kvf[dp, 64 + g * 16 : 64 + g * 16 + 16, b * 128 : b * 128 + 128] = ordered[
                b * 16 : b * 16 + 16, g * 128 : g * 128 + 128
            ]
    v_steps = ring([(kvf, 64, 64)], vsnd, vrcv)
    v_steps[0]()
    v_steps[1]()
    v_steps[2]()

    length = len_ref[0]
    factor = (DN + DR) ** -0.5 * math.log2(math.e)
    half = NB // 2
    chunk = ROWS // half

    def attend(r):
        for e in range(half):
            await_block(recv, a_sem, r * half + e)
        rows = recv[pl.ds(r * 16, 16)].reshape(chunk, WIDE)
        scores = mm(rows, kt[...]) * factor
        slot = iota((chunk, KEYS), 1)
        step = iota((chunk, 1), 0) % STEPS
        last = jnp.maximum(length - 1, 0)
        keep = (slot <= last) | ((slot >= CACHE) & (slot <= CACHE + step))
        scores = jnp.where(keep, scores, -1e30)
        top = jnp.max(scores, axis=1, keepdims=True)
        raised = jnp.exp2(scores - top)
        total = jnp.sum(raised, axis=1, keepdims=True)
        mixed = mm(raised.astype(BF), latx[...]) / total
        outs[pl.ds(r * 16, 16)] = mixed.astype(BF).reshape(16, 16, KVR)

        def one(j, c):
            t = r * 16 + j

            @pl.when(t != me)
            def _():
                pltpu.make_async_remote_copy(
                    outs.at[t], back.at[me], snd.at[4], o_sem.at[mine], here(t), MESH
                ).start()

            return c

        lax.fori_loop(0, 16, one, 0)

    first = me // 16

    def attend_one(k, carry):
        attend(lax.rem(first + k, half))
        return carry

    lax.fori_loop(0, half, attend_one, 0)
    own_o = pltpu.make_async_copy(outs.at[me], back.at[me], o_sem.at[mine])
    own_o.start()
    v_steps[3]()
    v_steps[4]()

    def collect(g, carry):
        await_block(back, o_sem, g)
        block = mm(by_head, back[pl.ds(g * BLOCK, BLOCK)].reshape(128, KVR)).astype(BF)
        for h in range(HEADS):
            lt[h, pl.ds(pl.multiple_of(g * 32, 32), 32), :] = block[h * 32 : h * 32 + 32]
        return carry

    lax.fori_loop(0, NB, collect, 0)
    for h in range(HEADS):
        values = kvf[:, 64:128, h * DV : (h + 1) * DV].reshape(KVR, DV)
        att[:, h * DV : (h + 1) * DV] = mm(lt[h], values).astype(BF)
    out_ref[...] = mm(by_step, att[...]).astype(BF).reshape(STEPS, GROUPS, HEADS * DV)

    def await_sent(ref, k):
        block = ref.at[pl.ds(0, GROUPS - 1)]
        pltpu.make_async_copy(block, block, snd.at[k]).wait()

    await_sent(rq, 0)
    await_sent(pack, 1)
    await_sent(packv, 2)
    await_sent(send, 3)
    await_sent(outs, 4)


def body(
    query_latent,
    query_weight,
    key_weight,
    value_weight,
    cache_latent,
    cache_rope,
    new_latent,
    new_rope,
    lengths,
):
    vmem = pl.BlockSpec(memory_space=pltpu.VMEM)
    anywhere = pl.BlockSpec(memory_space=pl.ANY)
    smem = pl.BlockSpec(memory_space=pltpu.SMEM)
    dma = pltpu.SemaphoreType.DMA
    return pl.pallas_call(
        kernel,
        out_shape=jax.ShapeDtypeStruct((STEPS, GROUPS, HEADS * DV), BF),
        in_specs=[vmem, vmem, vmem, vmem, anywhere, anywhere, vmem, vmem, smem],
        out_specs=vmem,
        scratch_shapes=[
            pltpu.VMEM((8, GROUPS * 768), F32),
            pltpu.VMEM((8, GROUPS * 512), F32),
            pltpu.VMEM((8, GROUPS * 512), F32),
            pltpu.VMEM((48, 128), F32),
            pltpu.VMEM((GROUPS, 48, 128), BF),
            pltpu.VMEM((GROUPS, 16, 128), BF),
            pltpu.VMEM((48, 128), BF),
            pltpu.VMEM((GROUPS, 48, 128), BF),
            pltpu.VMEM((GROUPS, 16, 128), BF),
            pltpu.VMEM((GROUPS, 48, 128), BF),
            pltpu.VMEM((128, QR), BF),
            pltpu.VMEM((DP, 192, 768), BF),
            pltpu.VMEM((DP, 128, 512), BF),
            pltpu.VMEM((ROWS, WIDE), BF),
            pltpu.VMEM((GROUPS, 16, WIDE), BF),
            pltpu.VMEM((GROUPS, 16, WIDE), BF),
            pltpu.VMEM((KEYS, KVR), BF),
            pltpu.VMEM((WIDE, KEYS), BF),
            pltpu.VMEM((GROUPS, 16, KVR), BF),
            pltpu.VMEM((GROUPS, 16, KVR), BF),
            pltpu.VMEM((HEADS, 128, KVR), BF),
            pltpu.VMEM((128, HEADS * DV), BF),
            dma((2,)),
            dma((5,)),
            dma((NB,)),
            dma((NB,)),
            dma((NB,)),
            dma((NB,)),
            dma((NB,)),
            dma((20,)),
            dma((20,)),
            dma((10,)),
            dma((10,)),
        ],
        compiler_params=pltpu.CompilerParams(
            collective_id=0, has_side_effects=True, vmem_limit_bytes=56 * 1024 * 1024
        ),
    )(
        query_latent.reshape(STEPS, QR),
        query_weight,
        key_weight,
        value_weight,
        cache_latent,
        cache_rope,
        new_latent.reshape(STEPS, KVR),
        new_rope.reshape(STEPS, DR),
        lengths,
    )


def solution(mesh):
    placed = (
        P(None, ("dp", "head"), None),
        P(("dp", "head"), None),
        P(("dp", "head"), None),
        P(("dp", "head"), None),
        P(("dp", "head"), None, None),
        P(("dp", "head"), None, None),
        P(None, ("dp", "head"), None),
        P(None, ("dp", "head"), None),
        P(("dp", "head")),
    )
    return jax.shard_map(
        body, mesh=mesh, in_specs=placed, out_specs=P(None, "dp", "head"), check_vma=False
    )
```

time: 841 us -> 86.2 us (0.10)
  the two profiles are of different devices: /device:TPU:1 before, /device:TPU:24 now
where the time goes in v1:
time: 86.2 us; the launch traced here: 86.1 us
  Pallas kernels  83.8 us (97%)
  local copies, waits for them, and re-layouts  1.57 us (2%)
    pallas_call x1, Pallas kernels, body(): pl.pallas_call(kernel, out_shape=jax.ShapeDtypeStruct((STEPS, GROUPS, HEA...  83.8 us

profile of v1, /device:TPU:24, one launch (start us, length us, event | category | flops | bytes accessed | tf_op | source)
XLA Modules:
  0.0 86.1 jit_solution(13835131105817882791)
XLA Ops:
  0.7 83.8 %shard_map.91 = bf16[4,32,512]{2,1,0:T(8,128)(2,1)} custom-call(bf16[4,1536]{1,0:T(4,128)(2,1)} %bitcast.3, bf16[6,24576]{1,0:T(8,128)(2,1)} %wq_ref.1, bf16[2,16384]{1,0:T(2,128)(2,1)} %kw_ref.1, bf16[2,16384]{1,0:T(2,128)(2,1)} %vw_ref.1, bf16[1,2048,512]{2,1,0:T(8,128)(2,1)} %lat_hbm.1, bf16[1,64,2048]{2,1,0:T(8,128)(2,1)} %rope_hbm.1, ...), custom_call_target="tpu_custom_call" | custom-call | tf_op jit(solution)/shard_map/pallas_call | solution.py:406
  84.5 1.6 %copy.12 = bf16[4,32,512]{2,1,0:T(8,128)(2,1)} copy(bf16[4,32,512]{2,1,0:T(8,128)(2,1)} %shard_map.91) | data formatting | bytes 262144

commit v2 on v1

v2 whole, which is shorter than its diff:
```python
import functools
import math

import jax
import jax.numpy as jnp
from jax import lax
from jax.experimental import pallas as pl
from jax.experimental.pallas import tpu as pltpu
from jax.sharding import PartitionSpec as P

QR = 1536
KVR = 512
DN = 128
DR = 64
DV = 128
CACHE = 2048
STEPS = 4
GROUPS = 32
HEADS = 4
RINGX = 4
RINGY = 4
RINGZ = 8
DP = 8
KEYS = CACHE + 128
WIDE = KVR + 128
ROWS = GROUPS * HEADS * STEPS
BLOCK = 8
NB = GROUPS // BLOCK
BF = jnp.bfloat16
F32 = jnp.float32
MESH = pl.DeviceIdType.MESH


def iota(shape, dim):
    return lax.broadcasted_iota(jnp.int32, shape, dim)


def one_hot(source, columns):
    rows = source.shape[0]
    return jnp.where(iota((rows, columns), 1) == source, 1.0, 0.0).astype(BF)


def mm(a, b):
    return jnp.dot(a, b, preferred_element_type=F32)


def mm_t(a, b):
    return lax.dot_general(a, b, (((1,), (1,)), ((), ())), preferred_element_type=F32)


def kernel(
    q_ref, wq_ref, kw_ref, vw_ref, lat_hbm, rope_hbm, nl_ref, nr_ref, len_ref, out_ref,
    w32, k32, v32, small, packa, packb, packv, qsend, rwa, rwb, rv, rq, qnat, wa, wb, ka, kb, vf,
    absq, posq, senda, sendb, recva, recvb, lhs, latx, kt, outs, back, lt, att,
    load_sem, snd, rcv, xsnd, xrcv, ysnd, yrcv, vsnd, vrcv,
):
    dp = lax.axis_index("dp")
    me = lax.axis_index("head")
    xpos = dp // 2
    core = dp % 2
    right = ((xpos + 1) % RINGX) * 2 + core
    left = ((xpos + RINGX - 1) % RINGX) * 2 + core
    across = ((xpos + 2) % RINGX) * 2 + core
    other = xpos * 2 + (1 - core)
    zpos = me // RINGY
    ypos = me % RINGY
    diagonal = (ypos + 2 * RINGY - zpos) % RINGY
    slot = diagonal * RINGZ + zpos

    def here(t):
        return {"dp": dp, "head": t}

    def peer(i):
        d = (diagonal + i // RINGZ) % RINGY
        z = (zpos + i) % RINGZ
        return d * RINGZ + z, z * RINGY + (d + z) % RINGY

    barrier = pltpu.get_barrier_semaphore()

    def greet(i, carry):
        pl.semaphore_signal(barrier, inc=1, device_id=here(peer(i)[1]), device_id_type=MESH)
        return carry

    lax.fori_loop(1, GROUPS, greet, 0)
    for d in (left, right, other):
        pl.semaphore_signal(barrier, inc=1, device_id={"dp": d, "head": me}, device_id_type=MESH)

    load_lat = pltpu.make_async_copy(lat_hbm.at[0], latx.at[pl.ds(0, CACHE)], load_sem.at[0])
    load_rope = pltpu.make_async_copy(rope_hbm.at[0], kt.at[pl.ds(KVR, DR), pl.ds(0, CACHE)], load_sem.at[1])
    load_lat.start()
    load_rope.start()

    w32[6:8, :] = jnp.zeros((2, w32.shape[1]), F32)
    w32[0:6, :] = wq_ref[...].astype(F32)
    k32[0:6, :] = jnp.zeros((6, k32.shape[1]), F32)
    k32[6:8, :] = kw_ref[...].astype(F32)

    def pack_weights(t, carry):
        wide = pl.multiple_of(t * 768, 128)
        narrow = pl.multiple_of(t * 512, 128)
        p = [w32[:, pl.ds(wide + b * 128, 128)] for b in range(6)]
        k = [k32[:, pl.ds(narrow + b * 128, 128)] for b in range(4)]
        low = iota((8, 128), 1) < DR
        positions = jnp.where(low, p[4], p[5])
        swapped = jnp.where(low, p[5], p[4])
        packa[t] = jnp.concatenate([p[0] + k[0], p[1] + k[1], p[2], positions], axis=0).astype(BF)
        packb[t] = jnp.concatenate([p[3] + k[2], swapped + k[3]], axis=0).astype(BF)
        return carry

    lax.fori_loop(0, GROUPS, pack_weights, 0)
    for j in range(QR // 128):
        small[4 * j : 4 * j + 4, :] = q_ref[:, 128 * j : 128 * j + 128].astype(F32)
    qsend[...] = small[...].astype(BF)
    for b in range(HEADS):
        v32[2 * b : 2 * b + 2, :] = vw_ref[...].astype(F32)

    def pack_values(t, carry):
        narrow = pl.multiple_of(t * 512, 128)
        row = iota((8, 128), 0) // 2
        value = jnp.zeros((8, 128), F32)
        for b in range(HEADS):
            value = jnp.where(row == b, v32[:, pl.ds(narrow + b * 128, 128)], value)
        packv[t] = jnp.concatenate([value, jnp.zeros((8, 128), F32)], axis=0).astype(BF)
        return carry

    lax.fori_loop(0, GROUPS, pack_values, 0)

    pl.semaphore_wait(barrier, GROUPS - 1 + 3)

    def scatter(source, target, k, place):
        def one(i, carry):
            s, t = peer(i)
            pltpu.make_async_remote_copy(
                source(s, t), target.at[place], snd.at[k], rcv.at[k], here(t), MESH
            ).start()
            return carry

        pltpu.make_async_copy(source(slot, me), target.at[place], rcv.at[k]).start()
        lax.fori_loop(1, GROUPS, one, 0)

    def arrive(target, k):
        pltpu.make_async_copy(target, target, rcv.at[k]).wait()

    scatter(lambda s, t: packa.at[t], rwa, 0, me)
    scatter(lambda s, t: packb.at[t], rwb, 1, me)
    scatter(lambda s, t: qsend, rq, 2, slot)
    scatter(lambda s, t: packv.at[t], rv, 3, me)

    small[0:8, :] = jnp.zeros((8, 128), F32)
    small[0:4, 0:DR] = nr_ref[...].astype(F32)
    fresh_rope = jnp.concatenate([small[0:8, :], jnp.zeros((120, 128), F32)], axis=0)
    kt[KVR:, CACHE:] = fresh_rope.T.astype(BF)
    kt[KVR + DR :, :CACHE] = jnp.zeros((128 - DR, CACHE), BF)
    for b in range(KVR // 128):
        small[0:8, :] = jnp.zeros((8, 128), F32)
        small[0:4, :] = nl_ref[:, b * 128 : b * 128 + 128].astype(F32)
        fresh = jnp.concatenate([small[0:8, :], jnp.zeros((120, 128), F32)], axis=0)
        latx[CACHE:, b * 128 : b * 128 + 128] = fresh.astype(BF)
    load_lat.wait()
    load_rope.wait()

    def turn(i, carry):
        at = pl.multiple_of(i * 128, 128)
        kt[0:KVR, pl.ds(at, 128)] = latx[pl.ds(at, 128), :].T
        return carry

    lax.fori_loop(0, KEYS // 128, turn, 0)

    def weight_order(blocks):
        o = iota((blocks * 64, 1), 0)
        u = o % 64
        sixth = (u * 43) >> 8
        from_query = sixth * (blocks * 8) + (o // 64) * 8 + (u - sixth * 6)
        from_key = ((u - 48) // 2) * (blocks * 8) + (o // 64) * 8 + 6 + (u % 2)
        return one_hot(jnp.where(u < 48, from_query, from_key), blocks * 64)

    order_a = weight_order(4)
    order_b = weight_order(2)
    o = iota((384, 1), 0)
    inside = o % 32
    q_order = one_hot((inside // 4) * 48 + (o // 32) * 4 + inside % 4, 384)
    o = iota((128, 1), 0)
    by_slot = one_hot(((o // 4) % 4) * 32 + (o // 16) * 4 + o % 4, 128)
    by_part = one_hot(((o // 4) % 8) * 16 + (o // 32) * 4 + o % 4, 128)
    halves = one_hot(((o // 8) % 8) * 16 + (o // 64) * 8 + o % 8, 128)
    unhalve = one_hot(((o // 8) % 2) * 64 + (o // 16) * 8 + o % 8, 128)
    sequence = o % 32
    home = ((sequence % 4 + 8 - sequence // 4) % 4) * 8 + sequence // 4
    by_step = one_hot(home * 4 + o // 32, 128)

    def rearranged(order, ref, rows):
        blocks = [ref[g * BLOCK : (g + 1) * BLOCK].reshape(BLOCK * rows, 128) for g in range(NB)]
        return mm(order, jnp.concatenate(blocks, axis=1)).astype(BF)

    def compact(order, ref, blocks, weights, keys):
        ordered = rearranged(order, ref, blocks * 8)
        for b in range(blocks):
            for g in range(NB):
                lanes = slice(g * 128, g * 128 + 128)
                weights[dp, g * 48 : g * 48 + 48, b * 128 : b * 128 + 128] = ordered[b * 64 : b * 64 + 48, lanes]
                if b < 2:
                    keys[dp, g * 16 : g * 16 + 16, b * 128 : b * 128 + 128] = ordered[b * 64 + 48 : b * 64 + 64, lanes]

    def ring(pieces, ssem, rsem):
        count = len(pieces)

        def copy(k, p, owner, to, part=None):
            ref = pieces[p]
            rows = ref.shape[1]
            first = 0
            if part is not None:
                rows = rows // 2
                first = part * rows
            view = ref.at[owner, pl.ds(first, rows)]
            at = k * count + p
            return pltpu.make_async_remote_copy(view, view, ssem.at[at], rsem.at[at], {"dp": to, "head": me}, MESH)

        every = range(count)

        def begin():
            for p in every:
                copy(0, p, dp, right, 0).start()
                copy(1, p, dp, left, 1).start()
            for p in every:
                copy(2, p, dp, right, 1).start()
                copy(3, p, dp, left, 0).start()
            for p in every:
                copy(4, p, dp, other).start()

        def forward():
            for p in every:
                copy(0, p, left, right, 0).wait_recv()
                copy(5, p, left, right, 0).start()
                copy(1, p, right, left, 1).wait_recv()
                copy(6, p, right, left, 1).start()

        def neighbours():
            for p in every:
                copy(2, p, left, right, 1).wait_recv()
                copy(7, p, left, other).start()
                copy(3, p, right, left, 0).wait_recv()
                copy(8, p, right, other).start()

        def far():
            for p in every:
                copy(5, p, across, right, 0).wait_recv()
                copy(6, p, across, left, 1).wait_recv()
                copy(9, p, across, other).start()

        def finish():
            sib = 1 - 2 * core
            for p in every:
                copy(4, p, dp + sib, other).wait_recv()
                copy(7, p, left + sib, other).wait_recv()
                copy(8, p, right + sib, other).wait_recv()
                copy(9, p, across + sib, other).wait_recv()

        def close():
            for p in every:
                for k, part in ((0, 0), (1, 1), (2, 1), (3, 0), (4, None), (5, 0), (6, 1), (7, None), (8, None), (9, None)):
                    copy(k, p, dp, right, part).wait_send()

        return begin, forward, neighbours, far, finish, close

    ring_a = ring([wa, ka], xsnd, xrcv)
    ring_b = ring([wb, kb], ysnd, yrcv)
    ring_v = ring([vf], vsnd, vrcv)

    arrive(rwa, 0)
    compact(order_a, rwa, 4, wa, ka)
    ring_a[0]()
    arrive(rwb, 1)
    compact(order_b, rwb, 2, wb, kb)
    ring_a[1]()
    ring_b[0]()
    ring_a[2]()

    arrive(rq, 2)
    ordered = rearranged(q_order, rq, 48)
    for j in range(QR // 128):
        for g in range(NB):
            qnat[g * 32 : g * 32 + 32, j * 128 : j * 128 + 128] = ordered[j * 32 : j * 32 + 32, g * 128 : g * 128 + 128]
    ring_a[3]()
    ring_a[4]()

    def absorb(h, plain, keys):
        lanes = slice((h % 2) * DN, (h % 2) * DN + DN)
        absq[h * 128 : h * 128 + 128, :] = mm_t(plain.astype(BF), keys[:, :, lanes].reshape(KVR, DN)).astype(BF)

    def spread(pair, with_position, send, recv, k):
        for d in range(NB):
            stacked = [
                absq[h * 128 + d * 32 : h * 128 + d * 32 + 32, e * 256 : e * 256 + 256]
                for e in range(2)
                for h in (2 * pair, 2 * pair + 1)
            ]
            stacked = jnp.concatenate(stacked, axis=0)
            if with_position:
                position = [posq[h * 128 + d * 32 : h * 128 + d * 32 + 32, :] for h in range(HEADS)]
                stacked = jnp.concatenate([stacked, jnp.concatenate(position, axis=0)], axis=1)
            send[d * BLOCK : (d + 1) * BLOCK] = mm(by_slot, stacked).astype(BF).reshape(BLOCK, 16, stacked.shape[1])
        scatter(lambda s, t: send.at[s], recv, k, slot)

    projected = mm(qnat[...], wa[...].reshape(QR, 512))
    absorb(0, projected[:, 0:128], ka)
    absorb(1, projected[:, 192:320], ka)
    posq[:, DR:] = jnp.zeros((ROWS, 128 - DR), BF)
    for h, at in enumerate((128, 320, 384, 448)):
        posq[h * 128 : h * 128 + 128, 0:DR] = projected[:, at : at + DR].astype(BF)
    spread(0, True, senda, recva, 4)

    for step in ring_b[1:5]:
        step()
    projected = mm(qnat[...], wb[...].reshape(QR, 256))
    absorb(2, projected[:, 0:128], kb)
    absorb(3, pltpu.roll(projected[:, 128:256], DR, 1), kb)
    spread(1, False, sendb, recvb, 5)

    o = iota((64, 1), 0)
    v_order = one_hot(((o % 16) // 2) * 16 + (o // 16) * 2 + o % 2, 128)
    arrive(rv, 3)
    ordered = rearranged(v_order, rv, 16)
    for b in range(4):
        for g in range(NB):
            vf[dp, g * 16 : g * 16 + 16, b * 128 : b * 128 + 128] = ordered[b * 16 : b * 16 + 16, g * 128 : g * 128 + 128]
    ring_v[0]()
    ring_v[1]()

    length = len_ref[0]
    factor = (DN + DR) ** -0.5 * math.log2(math.e)
    chunk = ROWS // 2

    def attend(pair):
        scores = mm(lhs[pair], kt[...]) * factor
        key = iota((chunk, KEYS), 1)
        step = iota((chunk, 1), 0) % STEPS
        last = jnp.maximum(length - 1, 0)
        keep = (key <= last) | ((key >= CACHE) & (key <= CACHE + step))
        scores = jnp.where(keep, scores, -1e30)
        top = jnp.max(scores, axis=1, keepdims=True)
        raised = jnp.exp2(scores - top)
        total = jnp.sum(raised, axis=1, keepdims=True)
        mixed = (mm(raised.astype(BF), latx[...]) / total).astype(BF)
        for d in range(NB):
            stacked = jnp.concatenate(
                [mixed[d * 64 : d * 64 + 64, 0:256], mixed[d * 64 : d * 64 + 64, 256:512]], axis=0
            )
            outs[pair, d * BLOCK : (d + 1) * BLOCK] = mm(unhalve, stacked).astype(BF).reshape(BLOCK, 16, 256)
        scatter(lambda s, t: outs.at[pair, s], back.at[pair], 6 + pair, slot)

    arrive(recva, 4)
    for d in range(NB):
        block = mm(halves, recva[d * BLOCK : (d + 1) * BLOCK].reshape(128, 384)).astype(BF)
        rows = slice(d * 64, d * 64 + 64)
        lhs[0, rows, 0:256] = block[0:64, 0:256]
        lhs[0, rows, 256:512] = block[64:128, 0:256]
        lhs[0, rows, 512:640] = block[0:64, 256:384]
        lhs[1, rows, 512:640] = block[64:128, 256:384]
    attend(0)
    ring_v[2]()
    ring_v[3]()
    arrive(recvb, 5)
    for d in range(NB):
        block = mm(halves, recvb[d * BLOCK : (d + 1) * BLOCK].reshape(128, 256)).astype(BF)
        rows = slice(d * 64, d * 64 + 64)
        lhs[1, rows, 0:256] = block[0:64]
        lhs[1, rows, 256:512] = block[64:128]
    attend(1)
    ring_v[4]()

    for pair in range(2):
        arrive(back.at[pair], 6 + pair)
        for d in range(NB):
            block = mm(by_part, back[pair, d * BLOCK : (d + 1) * BLOCK].reshape(128, 256)).astype(BF)
            for e in range(2):
                for h in range(2):
                    at = (e * 2 + h) * 32
                    lt[h, d * 32 : d * 32 + 32, e * 256 : e * 256 + 256] = block[at : at + 32]
        for h in range(2):
            lanes = slice((2 * pair + h) * DV, (2 * pair + h + 1) * DV)
            att[:, lanes] = mm(lt[h], vf[:, :, lanes].reshape(KVR, DV)).astype(BF)
    out_ref[...] = mm(by_step, att[...]).astype(BF).reshape(STEPS, GROUPS, HEADS * DV)

    for k, ref in enumerate((packa, packb, rq, packv, senda, sendb, outs.at[0], outs.at[1])):
        block = ref.at[pl.ds(0, GROUPS - 1)]
        pltpu.make_async_copy(block, block, snd.at[k]).wait()
    for steps in (ring_a, ring_b, ring_v):
        steps[5]()


def body(
    query_latent,
    query_weight,
    key_weight,
    value_weight,
    cache_latent,
    cache_rope,
    new_latent,
    new_rope,
    lengths,
):
    vmem = pl.BlockSpec(memory_space=pltpu.VMEM)
    anywhere = pl.BlockSpec(memory_space=pl.ANY)
    smem = pl.BlockSpec(memory_space=pltpu.SMEM)
    dma = pltpu.SemaphoreType.DMA
    return pl.pallas_call(
        kernel,
        out_shape=jax.ShapeDtypeStruct((STEPS, GROUPS, HEADS * DV), BF),
        in_specs=[vmem, vmem, vmem, vmem, anywhere, anywhere, vmem, vmem, smem],
        out_specs=vmem,
        scratch_shapes=[
            pltpu.VMEM((8, GROUPS * 768), F32),
            pltpu.VMEM((8, GROUPS * 512), F32),
            pltpu.VMEM((8, GROUPS * 512), F32),
            pltpu.VMEM((48, 128), F32),
            pltpu.VMEM((GROUPS, 32, 128), BF),
            pltpu.VMEM((GROUPS, 16, 128), BF),
            pltpu.VMEM((GROUPS, 16, 128), BF),
            pltpu.VMEM((48, 128), BF),
            pltpu.VMEM((GROUPS, 32, 128), BF),
            pltpu.VMEM((GROUPS, 16, 128), BF),
            pltpu.VMEM((GROUPS, 16, 128), BF),
            pltpu.VMEM((GROUPS, 48, 128), BF),
            pltpu.VMEM((128, QR), BF),
            pltpu.VMEM((DP, 192, 512), BF),
            pltpu.VMEM((DP, 192, 256), BF),
            pltpu.VMEM((DP, 64, 256), BF),
            pltpu.VMEM((DP, 64, 256), BF),
            pltpu.VMEM((DP, 64, 512), BF),
            pltpu.VMEM((ROWS, KVR), BF),
            pltpu.VMEM((ROWS, 128), BF),
            pltpu.VMEM((GROUPS, 16, 384), BF),
            pltpu.VMEM((GROUPS, 16, 256), BF),
            pltpu.VMEM((GROUPS, 16, 384), BF),
            pltpu.VMEM((GROUPS, 16, 256), BF),
            pltpu.VMEM((2, ROWS // 2, WIDE), BF),
            pltpu.VMEM((KEYS, KVR), BF),
            pltpu.VMEM((WIDE, KEYS), BF),
            pltpu.VMEM((2, GROUPS, 16, 256), BF),
            pltpu.VMEM((2, GROUPS, 16, 256), BF),
            pltpu.VMEM((2, 128, KVR), BF),
            pltpu.VMEM((128, HEADS * DV), BF),
            dma((2,)),
            dma((8,)),
            dma((8,)),
            dma((20,)),
            dma((20,)),
            dma((20,)),
            dma((20,)),
            dma((10,)),
            dma((10,)),
        ],
        compiler_params=pltpu.CompilerParams(
            collective_id=0, has_side_effects=True, vmem_limit_bytes=56 * 1024 * 1024
        ),
    )(
        query_latent.reshape(STEPS, QR),
        query_weight,
        key_weight,
        value_weight,
        cache_latent,
        cache_rope,
        new_latent.reshape(STEPS, KVR),
        new_rope.reshape(STEPS, DR),
        lengths,
    )


def solution(mesh):
    placed = (
        P(None, ("dp", "head"), None),
        P(("dp", "head"), None),
        P(("dp", "head"), None),
        P(("dp", "head"), None),
        P(("dp", "head"), None, None),
        P(("dp", "head"), None, None),
        P(None, ("dp", "head"), None),
        P(None, ("dp", "head"), None),
        P(("dp", "head")),
    )
    return jax.shard_map(
        body, mesh=mesh, in_specs=placed, out_specs=P(None, "dp", "head"), check_vma=False
    )
```

time: 86.2 us -> 70.1 us (0.81)
  the two profiles are of different devices: /device:TPU:24 before, /device:TPU:1 now
where the time goes in v2:
time: 70.1 us; the launch traced here: 70 us
  Pallas kernels  67.8 us (97%)
  local copies, waits for them, and re-layouts  1.57 us (2%)
    pallas_call x1, Pallas kernels, body(): pl.pallas_call(kernel, out_shape=jax.ShapeDtypeStruct((STEPS, GROUPS, HEA...  67.8 us
    unnamed x1, local copies, waits for them, and re-layouts  1.57 us

profile of v2, /device:TPU:1, one launch (start us, length us, event | category | flops | bytes accessed | tf_op | source)
XLA Modules:
  0.0 70.0 jit_solution(1802491536681516699)
XLA Ops:
  0.7 67.8 %shard_map.91 = bf16[4,32,512]{2,1,0:T(8,128)(2,1)} custom-call(bf16[4,1536]{1,0:T(4,128)(2,1)} %bitcast.3, bf16[6,24576]{1,0:T(8,128)(2,1)} %wq_ref.1, bf16[2,16384]{1,0:T(2,128)(2,1)} %kw_ref.1, bf16[2,16384]{1,0:T(2,128)(2,1)} %vw_ref.1, bf16[1,2048,512]{2,1,0:T(8,128)(2,1)} %lat_hbm.1, bf16[1,64,2048]{2,1,0:T(8,128)(2,1)} %rope_hbm.1, ...), custom_call_target="tpu_custom_call" | custom-call | tf_op jit(solution)/shard_map/pallas_call | solution.py:406
  68.4 1.6 %copy.12 = bf16[4,32,512]{2,1,0:T(8,128)(2,1)} copy(bf16[4,32,512]{2,1,0:T(8,128)(2,1)} %shard_map.91) | data formatting | bytes 262144

commit v3 on v2

--- a/solution.py
+++ b/solution.py
@@ -50,9 +50,9 @@
 
 def kernel(
     q_ref, wq_ref, kw_ref, vw_ref, lat_hbm, rope_hbm, nl_ref, nr_ref, len_ref, out_ref,
-    w32, k32, v32, small, packa, packb, packv, qsend, rwa, rwb, rv, rq, qnat, wa, wb, ka, kb, vf,
-    absq, posq, senda, sendb, recva, recvb, lhs, latx, kt, outs, back, lt, att,
-    load_sem, snd, rcv, xsnd, xrcv, ysnd, yrcv, vsnd, vrcv,
+    w32, k32, v32, small, packr, packa, packb, packv, qsend, rwr, rwa, rwb, rv, rq, qnat, wr, wa, wb, ka, kb, vf,
+    absq, posq, sendr, senda, sendb, recvr, recva, recvb, lhs, latx, kt, outs, back, lt, att,
+    load_sem, snd, rcv, rrcvd, arcvd, brcvd, qsnd, qrcv, rsnd, rrcv, xsnd, xrcv, ysnd, yrcv, vsnd, vrcv,
 ):
     dp = lax.axis_index("dp")
     me = lax.axis_index("head")
@@ -70,18 +70,14 @@
     def here(t):
         return {"dp": dp, "head": t}
 
-    def peer(i):
-        d = (diagonal + i // RINGZ) % RINGY
-        z = (zpos + i) % RINGZ
-        return d * RINGZ + z, z * RINGY + (d + z) % RINGY
+    turns = [lax.rem(diagonal + k, RINGY) for k in range(RINGY)]
+    planes = [lax.rem(zpos + i, RINGZ) for i in range(RINGZ)]
+    partners = [(d * RINGZ + z, z * RINGY + lax.rem(d + z, RINGY)) for d in turns for z in planes]
 
     barrier = pltpu.get_barrier_semaphore()
 
-    def greet(i, carry):
-        pl.semaphore_signal(barrier, inc=1, device_id=here(peer(i)[1]), device_id_type=MESH)
-        return carry
-
-    lax.fori_loop(1, GROUPS, greet, 0)
+    for _, t in partners[1:]:
+        pl.semaphore_signal(barrier, inc=1, device_id=here(t), device_id_type=MESH)
     for d in (left, right, other):
         pl.semaphore_signal(barrier, inc=1, device_id={"dp": d, "head": me}, device_id_type=MESH)
 
@@ -103,7 +99,10 @@
         low = iota((8, 128), 1) < DR
         positions = jnp.where(low, p[4], p[5])
         swapped = jnp.where(low, p[5], p[4])
-        packa[t] = jnp.concatenate([p[0] + k[0], p[1] + k[1], p[2], positions], axis=0).astype(BF)
+        first = jnp.where(low, p[1], p[2])
+        exchanged = jnp.where(low, p[2], p[1])
+        packr[t] = jnp.concatenate([first, positions], axis=0).astype(BF)
+        packa[t] = jnp.concatenate([p[0] + k[0], exchanged + k[1]], axis=0).astype(BF)
         packb[t] = jnp.concatenate([p[3] + k[2], swapped + k[3]], axis=0).astype(BF)
         return carry
 
@@ -127,24 +126,34 @@
 
     pl.semaphore_wait(barrier, GROUPS - 1 + 3)
 
-    def scatter(source, target, k, place):
-        def one(i, carry):
-            s, t = peer(i)
-            pltpu.make_async_remote_copy(
-                source(s, t), target.at[place], snd.at[k], rcv.at[k], here(t), MESH
-            ).start()
-            return carry
-
-        pltpu.make_async_copy(source(slot, me), target.at[place], rcv.at[k]).start()
-        lax.fori_loop(1, GROUPS, one, 0)
+    def scatter(source, target, k, place, arrived, which=range(GROUPS)):
+        for i in which:
+            s, t = partners[i]
+            if i == 0:
+                pltpu.make_async_copy(source(slot, me), target.at[place], arrived(0)).start()
+            else:
+                pltpu.make_async_remote_copy(
+                    source(s, t), target.at[place], snd.at[k], arrived(i // BLOCK), here(t), MESH
+                ).start()
 
     def arrive(target, k):
         pltpu.make_async_copy(target, target, rcv.at[k]).wait()
 
-    scatter(lambda s, t: packa.at[t], rwa, 0, me)
-    scatter(lambda s, t: packb.at[t], rwb, 1, me)
-    scatter(lambda s, t: qsend, rq, 2, slot)
-    scatter(lambda s, t: packv.at[t], rv, 3, me)
+    def q_first(i):
+        to = ((zpos + i) % RINGZ) * RINGY + ypos
+        return pltpu.make_async_remote_copy(qsend, rq.at[ypos, zpos], qsnd.at[i - 1], qrcv.at[0], here(to), MESH)
+
+    def q_second(i):
+        to = zpos * RINGY + (ypos + i) % RINGY
+        return pltpu.make_async_remote_copy(
+            rq.at[ypos], rq.at[ypos], qsnd.at[RINGZ - 2 + i], qrcv.at[i], here(to), MESH
+        )
+
+    scatter(lambda s, t: packa.at[t], rwa, 0, me, lambda c: rcv.at[0])
+    pltpu.make_async_copy(qsend, rq.at[ypos, zpos], qrcv.at[0]).start()
+    for i in range(1, RINGZ):
+        q_first(i).start()
+    scatter(lambda s, t: packr.at[t], rwr, 2, me, lambda c: rcv.at[2])
 
     small[0:8, :] = jnp.zeros((8, 128), F32)
     small[0:4, 0:DR] = nr_ref[...].astype(F32)
@@ -174,8 +183,7 @@
         from_key = ((u - 48) // 2) * (blocks * 8) + (o // 64) * 8 + 6 + (u % 2)
         return one_hot(jnp.where(u < 48, from_query, from_key), blocks * 64)
 
-    order_a = weight_order(4)
-    order_b = weight_order(2)
+    w_order = weight_order(2)
     o = iota((384, 1), 0)
     inside = o % 32
     q_order = one_hot((inside // 4) * 48 + (o // 32) * 4 + inside % 4, 384)
@@ -188,17 +196,20 @@
     home = ((sequence % 4 + 8 - sequence // 4) % 4) * 8 + sequence // 4
     by_step = one_hot(home * 4 + o // 32, 128)
 
-    def rearranged(order, ref, rows):
-        blocks = [ref[g * BLOCK : (g + 1) * BLOCK].reshape(BLOCK * rows, 128) for g in range(NB)]
+    def rearranged(order, blocks):
+        blocks = [block.reshape(order.shape[1], 128) for block in blocks]
         return mm(order, jnp.concatenate(blocks, axis=1)).astype(BF)
 
-    def compact(order, ref, blocks, weights, keys):
-        ordered = rearranged(order, ref, blocks * 8)
-        for b in range(blocks):
+    def eights(ref):
+        return [ref[g * BLOCK : (g + 1) * BLOCK] for g in range(NB)]
+
+    def compact(ref, weights, keys=None):
+        ordered = rearranged(w_order, eights(ref))
+        for b in range(2):
             for g in range(NB):
                 lanes = slice(g * 128, g * 128 + 128)
                 weights[dp, g * 48 : g * 48 + 48, b * 128 : b * 128 + 128] = ordered[b * 64 : b * 64 + 48, lanes]
-                if b < 2:
+                if keys is not None:
                     keys[dp, g * 16 : g * 16 + 16, b * 128 : b * 128 + 128] = ordered[b * 64 + 48 : b * 64 + 64, lanes]
 
     def ring(pieces, ssem, rsem):
@@ -221,6 +232,8 @@
             for p in every:
                 copy(0, p, dp, right, 0).start()
                 copy(1, p, dp, left, 1).start()
+
+        def begin_rest():
             for p in every:
                 copy(2, p, dp, right, 1).start()
                 copy(3, p, dp, left, 0).start()
@@ -260,78 +273,114 @@
                 for k, part in ((0, 0), (1, 1), (2, 1), (3, 0), (4, None), (5, 0), (6, 1), (7, None), (8, None), (9, None)):
                     copy(k, p, dp, right, part).wait_send()
 
-        return begin, forward, neighbours, far, finish, close
-
+        return begin, begin_rest, forward, neighbours, far, finish, close
+
+    BEGIN, REST, FORWARD, NEIGHBOURS, FAR, FINISH, CLOSE = range(7)
+    ring_r = ring([wr], rsnd, rrcv)
     ring_a = ring([wa, ka], xsnd, xrcv)
     ring_b = ring([wb, kb], ysnd, yrcv)
     ring_v = ring([vf], vsnd, vrcv)
 
     arrive(rwa, 0)
-    compact(order_a, rwa, 4, wa, ka)
-    ring_a[0]()
+    compact(rwa, wa, ka)
+    ring_a[BEGIN]()
+    ring_a[REST]()
+    eight = rq.at[ypos]
+    pltpu.make_async_copy(eight, eight, qrcv.at[0]).wait()
+    for i in range(1, RINGY):
+        q_second(i).start()
+    scatter(lambda s, t: packb.at[t], rwb, 1, me, lambda c: rcv.at[1])
+    scatter(lambda s, t: packv.at[t], rv, 3, me, lambda c: rcv.at[3])
+    arrive(rwr, 2)
+    compact(rwr, wr)
+    ring_r[BEGIN]()
+    ring_a[FORWARD]()
+    ring_r[REST]()
     arrive(rwb, 1)
-    compact(order_b, rwb, 2, wb, kb)
-    ring_a[1]()
-    ring_b[0]()
-    ring_a[2]()
-
-    arrive(rq, 2)
-    ordered = rearranged(q_order, rq, 48)
+    compact(rwb, wb, kb)
+    ring_b[BEGIN]()
+    ring_a[NEIGHBOURS]()
+    ring_r[FORWARD]()
+    ring_b[REST]()
+
+    for i in range(1, RINGY):
+        q_second(i).wait_recv()
+    ordered = rearranged(
+        q_order,
+        [jnp.concatenate([rq[(d + z) % RINGY, z] for z in range(RINGZ)], axis=0) for d in range(RINGY)],
+    )
     for j in range(QR // 128):
         for g in range(NB):
             qnat[g * 32 : g * 32 + 32, j * 128 : j * 128 + 128] = ordered[j * 32 : j * 32 + 32, g * 128 : g * 128 + 128]
-    ring_a[3]()
-    ring_a[4]()
-
-    def absorb(h, plain, keys):
-        lanes = slice((h % 2) * DN, (h % 2) * DN + DN)
-        absq[h * 128 : h * 128 + 128, :] = mm_t(plain.astype(BF), keys[:, :, lanes].reshape(KVR, DN)).astype(BF)
-
-    def spread(pair, with_position, send, recv, k):
-        for d in range(NB):
-            stacked = [
-                absq[h * 128 + d * 32 : h * 128 + d * 32 + 32, e * 256 : e * 256 + 256]
-                for e in range(2)
-                for h in (2 * pair, 2 * pair + 1)
-            ]
-            stacked = jnp.concatenate(stacked, axis=0)
-            if with_position:
-                position = [posq[h * 128 + d * 32 : h * 128 + d * 32 + 32, :] for h in range(HEADS)]
-                stacked = jnp.concatenate([stacked, jnp.concatenate(position, axis=0)], axis=1)
-            send[d * BLOCK : (d + 1) * BLOCK] = mm(by_slot, stacked).astype(BF).reshape(BLOCK, 16, stacked.shape[1])
-        scatter(lambda s, t: send.at[s], recv, k, slot)
-
-    projected = mm(qnat[...], wa[...].reshape(QR, 512))
-    absorb(0, projected[:, 0:128], ka)
-    absorb(1, projected[:, 192:320], ka)
+    ring_a[FAR]()
+    ring_a[FINISH]()
+
+    def spread(parts, send, recv, k, sems):
+        for c in range(NB):
+            d = turns[c]
+            rows = [ref[pl.ds(pl.multiple_of(at + d * 32, 32), 32), lanes] for ref, at, lanes in parts]
+            block = mm(by_slot, jnp.concatenate(rows, axis=0)).astype(BF)
+            send[pl.ds(d * BLOCK, BLOCK)] = block.reshape(BLOCK, 16, block.shape[1])
+            scatter(
+                lambda s, t: send.at[s], recv, k, slot, lambda c: sems.at[c], range(c * BLOCK, c * BLOCK + BLOCK)
+            )
+
+    def absorb(pair, weights, keys, send, recv, k, sems):
+        projected = mm(qnat[...], weights[...].reshape(QR, 256))
+        plain = (projected[:, 0:128], pltpu.roll(projected[:, 128:256], DR, 1))
+        for h in range(2):
+            lanes = slice(h * DN, h * DN + DN)
+            absq[h * 128 : h * 128 + 128, :] = mm_t(
+                plain[h].astype(BF), keys[:, :, lanes].reshape(KVR, DN)
+            ).astype(BF)
+        parts = [(absq, h * 128, slice(e * 256, e * 256 + 256)) for e in range(2) for h in range(2)]
+        spread(parts, send, recv, k, sems)
+
+    absorb(0, wa, ka, senda, recva, 4, arcvd)
+    ring_r[NEIGHBOURS]()
+    ring_b[FORWARD]()
+    ring_r[FAR]()
+    ring_r[FINISH]()
+
+    projected = mm(qnat[...], wr[...].reshape(QR, 256))
     posq[:, DR:] = jnp.zeros((ROWS, 128 - DR), BF)
-    for h, at in enumerate((128, 320, 384, 448)):
-        posq[h * 128 : h * 128 + 128, 0:DR] = projected[:, at : at + DR].astype(BF)
-    spread(0, True, senda, recva, 4)
-
-    for step in ring_b[1:5]:
+    for h in range(HEADS):
+        posq[h * 128 : h * 128 + 128, 0:DR] = projected[:, h * DR : h * DR + DR].astype(BF)
+    spread([(posq, h * 128, slice(None)) for h in range(HEADS)], sendr, recvr, 8, rrcvd)
+    for step in ring_b[NEIGHBOURS:CLOSE]:
         step()
-    projected = mm(qnat[...], wb[...].reshape(QR, 256))
-    absorb(2, projected[:, 0:128], kb)
-    absorb(3, pltpu.roll(projected[:, 128:256], DR, 1), kb)
-    spread(1, False, sendb, recvb, 5)
+    absorb(1, wb, kb, sendb, recvb, 5, brcvd)
 
     o = iota((64, 1), 0)
     v_order = one_hot(((o % 16) // 2) * 16 + (o // 16) * 2 + o % 2, 128)
     arrive(rv, 3)
-    ordered = rearranged(v_order, rv, 16)
+    ordered = rearranged(v_order, eights(rv))
     for b in range(4):
         for g in range(NB):
             vf[dp, g * 16 : g * 16 + 16, b * 128 : b * 128 + 128] = ordered[b * 16 : b * 16 + 16, g * 128 : g * 128 + 128]
-    ring_v[0]()
-    ring_v[1]()
+    ring_v[BEGIN]()
+    ring_v[REST]()
+    ring_v[FORWARD]()
 
     length = len_ref[0]
     factor = (DN + DR) ** -0.5 * math.log2(math.e)
-    chunk = ROWS // 2
-
-    def attend(pair):
-        scores = mm(lhs[pair], kt[...]) * factor
+    chunk = ROWS // 4
+
+    def attend(pair, half, recv, sems):
+        classes = [lax.rem(diagonal + NB - c, NB) for c in (2 * half, 2 * half + 1)]
+        for e, d in enumerate(classes):
+            rows = slice(e * 64, e * 64 + 64)
+            mine = pl.ds(d * BLOCK, BLOCK)
+            if pair == 0:
+                pltpu.make_async_copy(recvr.at[mine], recvr.at[mine], rrcvd.at[2 * half + e]).wait()
+                block = mm(halves, recvr[mine].reshape(128, 128)).astype(BF)
+                lhs[half, rows, 512:640] = block[0:64]
+                lhs[2 + half, rows, 512:640] = block[64:128]
+            pltpu.make_async_copy(recv.at[mine], recv.at[mine], sems.at[2 * half + e]).wait()
+            block = mm(halves, recv[mine].reshape(128, 256)).astype(BF)
+            lhs[2 * pair + half, rows, 0:256] = block[0:64]
+            lhs[2 * pair + half, rows, 256:512] = block[64:128]
+        scores = mm(lhs[2 * pair + half], kt[...]) * factor
         key = iota((chunk, KEYS), 1)
         step = iota((chunk, 1), 0) % STEPS
         last = jnp.maximum(length - 1, 0)
@@ -341,32 +390,24 @@
         raised = jnp.exp2(scores - top)
         total = jnp.sum(raised, axis=1, keepdims=True)
         mixed = (mm(raised.astype(BF), latx[...]) / total).astype(BF)
-        for d in range(NB):
+        for e, d in enumerate(classes):
             stacked = jnp.concatenate(
-                [mixed[d * 64 : d * 64 + 64, 0:256], mixed[d * 64 : d * 64 + 64, 256:512]], axis=0
+                [mixed[e * 64 : e * 64 + 64, 0:256], mixed[e * 64 : e * 64 + 64, 256:512]], axis=0
             )
-            outs[pair, d * BLOCK : (d + 1) * BLOCK] = mm(unhalve, stacked).astype(BF).reshape(BLOCK, 16, 256)
-        scatter(lambda s, t: outs.at[pair, s], back.at[pair], 6 + pair, slot)
-
-    arrive(recva, 4)
-    for d in range(NB):
-        block = mm(halves, recva[d * BLOCK : (d + 1) * BLOCK].reshape(128, 384)).astype(BF)
-        rows = slice(d * 64, d * 64 + 64)
-        lhs[0, rows, 0:256] = block[0:64, 0:256]
-        lhs[0, rows, 256:512] = block[64:128, 0:256]
-        lhs[0, rows, 512:640] = block[0:64, 256:384]
-        lhs[1, rows, 512:640] = block[64:128, 256:384]
-    attend(0)
-    ring_v[2]()
-    ring_v[3]()
-    arrive(recvb, 5)
-    for d in range(NB):
-        block = mm(halves, recvb[d * BLOCK : (d + 1) * BLOCK].reshape(128, 256)).astype(BF)
-        rows = slice(d * 64, d * 64 + 64)
-        lhs[1, rows, 0:256] = block[0:64]
-        lhs[1, rows, 256:512] = block[64:128]
-    attend(1)
-    ring_v[4]()
+            outs[pair, pl.ds(d * BLOCK, BLOCK)] = mm(unhalve, stacked).astype(BF).reshape(BLOCK, 16, 256)
+            turn_back = (NB - 2 * half - e) % NB
+            scatter(
+                lambda s, t: outs.at[pair, s], back.at[pair], 6 + pair, slot, lambda c: rcv.at[6 + pair],
+                range(turn_back * BLOCK, turn_back * BLOCK + BLOCK),
+            )
+
+    attend(0, 0, recva, arcvd)
+    ring_v[NEIGHBOURS]()
+    attend(0, 1, recva, arcvd)
+    ring_v[FAR]()
+    attend(1, 0, recvb, brcvd)
+    attend(1, 1, recvb, brcvd)
+    ring_v[FINISH]()
 
     for pair in range(2):
         arrive(back.at[pair], 6 + pair)
@@ -381,11 +422,15 @@
             att[:, lanes] = mm(lt[h], vf[:, :, lanes].reshape(KVR, DV)).astype(BF)
     out_ref[...] = mm(by_step, att[...]).astype(BF).reshape(STEPS, GROUPS, HEADS * DV)
 
-    for k, ref in enumerate((packa, packb, rq, packv, senda, sendb, outs.at[0], outs.at[1])):
+    for k, ref in enumerate((packa, packb, packr, packv, senda, sendb, outs.at[0], outs.at[1], sendr)):
         block = ref.at[pl.ds(0, GROUPS - 1)]
         pltpu.make_async_copy(block, block, snd.at[k]).wait()
-    for steps in (ring_a, ring_b, ring_v):
-        steps[5]()
+    for i in range(1, RINGZ):
+        q_first(i).wait_send()
+    for i in range(1, RINGY):
+        q_second(i).wait_send()
+    for steps in (ring_r, ring_a, ring_b, ring_v):
+        steps[CLOSE]()
 
 
 def body(
@@ -413,27 +458,32 @@
             pltpu.VMEM((8, GROUPS * 512), F32),
             pltpu.VMEM((8, GROUPS * 512), F32),
             pltpu.VMEM((48, 128), F32),
-            pltpu.VMEM((GROUPS, 32, 128), BF),
+            pltpu.VMEM((GROUPS, 16, 128), BF),
+            pltpu.VMEM((GROUPS, 16, 128), BF),
             pltpu.VMEM((GROUPS, 16, 128), BF),
             pltpu.VMEM((GROUPS, 16, 128), BF),
             pltpu.VMEM((48, 128), BF),
-            pltpu.VMEM((GROUPS, 32, 128), BF),
-            pltpu.VMEM((GROUPS, 16, 128), BF),
-            pltpu.VMEM((GROUPS, 16, 128), BF),
-            pltpu.VMEM((GROUPS, 48, 128), BF),
+            pltpu.VMEM((GROUPS, 16, 128), BF),
+            pltpu.VMEM((GROUPS, 16, 128), BF),
+            pltpu.VMEM((GROUPS, 16, 128), BF),
+            pltpu.VMEM((GROUPS, 16, 128), BF),
+            pltpu.VMEM((RINGY, RINGZ, 48, 128), BF),
             pltpu.VMEM((128, QR), BF),
-            pltpu.VMEM((DP, 192, 512), BF),
+            pltpu.VMEM((DP, 192, 256), BF),
+            pltpu.VMEM((DP, 192, 256), BF),
             pltpu.VMEM((DP, 192, 256), BF),
             pltpu.VMEM((DP, 64, 256), BF),
             pltpu.VMEM((DP, 64, 256), BF),
             pltpu.VMEM((DP, 64, 512), BF),
-            pltpu.VMEM((ROWS, KVR), BF),
+            pltpu.VMEM((ROWS // 2, KVR), BF),
             pltpu.VMEM((ROWS, 128), BF),
-            pltpu.VMEM((GROUPS, 16, 384), BF),
+            pltpu.VMEM((GROUPS, 16, 128), BF),
             pltpu.VMEM((GROUPS, 16, 256), BF),
-            pltpu.VMEM((GROUPS, 16, 384), BF),
             pltpu.VMEM((GROUPS, 16, 256), BF),
-            pltpu.VMEM((2, ROWS // 2, WIDE), BF),
+            pltpu.VMEM((GROUPS, 16, 128), BF),
+            pltpu.VMEM((GROUPS, 16, 256), BF),
+            pltpu.VMEM((GROUPS, 16, 256), BF),
+            pltpu.VMEM((4, ROWS // 4, WIDE), BF),
             pltpu.VMEM((KEYS, KVR), BF),
             pltpu.VMEM((WIDE, KEYS), BF),
             pltpu.VMEM((2, GROUPS, 16, 256), BF),
@@ -441,8 +491,15 @@
             pltpu.VMEM((2, 128, KVR), BF),
             pltpu.VMEM((128, HEADS * DV), BF),
             dma((2,)),
-            dma((8,)),
-            dma((8,)),
+            dma((9,)),
+            dma((9,)),
+            dma((NB,)),
+            dma((NB,)),
+            dma((NB,)),
+            dma((10,)),
+            dma((4,)),
+            dma((10,)),
+            dma((10,)),
             dma((20,)),
             dma((20,)),
             dma((20,)),

time: 70.1 us -> 67.5 us (0.963)
  Pallas kernels: 67.8 us -> 65.2 us
    pallas_call x1, Pallas kernels: 67.8 us -> 65.2 us  [body(): pl.pallas_call(kernel, out_shape=jax.ShapeDtypeStruct((STEPS, GROUPS, HEA...]
where the time goes in v3:
time: 67.5 us; the launch traced here: 67.4 us
  Pallas kernels  65.2 us (97%)
  local copies, waits for them, and re-layouts  1.57 us (2%)
    pallas_call x1, Pallas kernels, body(): pl.pallas_call(kernel, out_shape=jax.ShapeDtypeStruct((STEPS, GROUPS, HEA...  65.2 us
    unnamed x1, local copies, waits for them, and re-layouts  1.57 us

profile of v3, /device:TPU:1, one launch (start us, length us, event | category | flops | bytes accessed | tf_op | source)
XLA Modules:
  0.0 67.4 jit_solution(10740162219078060072)
XLA Ops:
  0.7 65.2 %shard_map.91 = bf16[4,32,512]{2,1,0:T(8,128)(2,1)} custom-call(bf16[4,1536]{1,0:T(4,128)(2,1)} %bitcast.3, bf16[6,24576]{1,0:T(8,128)(2,1)} %wq_ref.1, bf16[2,16384]{1,0:T(2,128)(2,1)} %kw_ref.1, bf16[2,16384]{1,0:T(2,128)(2,1)} %vw_ref.1, bf16[1,2048,512]{2,1,0:T(8,128)(2,1)} %lat_hbm.1, bf16[1,64,2048]{2,1,0:T(8,128)(2,1)} %rope_hbm.1, ...), custom_call_target="tpu_custom_call" | custom-call | tf_op jit(solution)/shard_map/pallas_call | solution.py:451
  65.8 1.6 %copy.12 = bf16[4,32,512]{2,1,0:T(8,128)(2,1)} copy(bf16[4,32,512]{2,1,0:T(8,128)(2,1)} %shard_map.91) | data formatting | bytes 262144

commit v4 on v3

--- a/solution.py
+++ b/solution.py
@@ -27,6 +27,14 @@
 BLOCK = 8
 NB = GROUPS // BLOCK
 BF = jnp.bfloat16
+
+
+def hops(i):
+    z, y = i % RINGZ, (i // RINGZ + i) % RINGY
+    return min(z, RINGZ - z) + min(y, RINGY - y)
+
+
+FAR_FIRST = sorted(range(GROUPS), key=lambda i: -hops(i))
 F32 = jnp.float32
 MESH = pl.DeviceIdType.MESH
 
@@ -76,7 +84,7 @@
 
     barrier = pltpu.get_barrier_semaphore()
 
-    for _, t in partners[1:]:
+    for _, t in [partners[i] for i in FAR_FIRST if i > 0]:
         pl.semaphore_signal(barrier, inc=1, device_id=here(t), device_id_type=MESH)
     for d in (left, right, other):
         pl.semaphore_signal(barrier, inc=1, device_id={"dp": d, "head": me}, device_id_type=MESH)
@@ -126,8 +134,8 @@
 
     pl.semaphore_wait(barrier, GROUPS - 1 + 3)
 
-    def scatter(source, target, k, place, arrived, which=range(GROUPS)):
-        for i in which:
+    def scatter(source, target, k, place, arrived, which=FAR_FIRST):
+        for i in sorted(which, key=lambda i: -hops(i)):
             s, t = partners[i]
             if i == 0:
                 pltpu.make_async_copy(source(slot, me), target.at[place], arrived(0)).start()
@@ -151,7 +159,7 @@
 
     scatter(lambda s, t: packa.at[t], rwa, 0, me, lambda c: rcv.at[0])
     pltpu.make_async_copy(qsend, rq.at[ypos, zpos], qrcv.at[0]).start()
-    for i in range(1, RINGZ):
+    for i in (4, 3, 5, 2, 6, 1, 7):
         q_first(i).start()
     scatter(lambda s, t: packr.at[t], rwr, 2, me, lambda c: rcv.at[2])
 
@@ -296,13 +304,13 @@
     ring_r[BEGIN]()
     ring_a[FORWARD]()
     ring_r[REST]()
+    ring_r[FORWARD]()
+    ring_a[NEIGHBOURS]()
+    ring_a[FAR]()
     arrive(rwb, 1)
     compact(rwb, wb, kb)
     ring_b[BEGIN]()
-    ring_a[NEIGHBOURS]()
-    ring_r[FORWARD]()
     ring_b[REST]()
-
     for i in range(1, RINGY):
         q_second(i).wait_recv()
     ordered = rearranged(
@@ -312,8 +320,8 @@
     for j in range(QR // 128):
         for g in range(NB):
             qnat[g * 32 : g * 32 + 32, j * 128 : j * 128 + 128] = ordered[j * 32 : j * 32 + 32, g * 128 : g * 128 + 128]
-    ring_a[FAR]()
     ring_a[FINISH]()
+    ring_r[NEIGHBOURS]()
 
     def spread(parts, send, recv, k, sems):
         for c in range(NB):
@@ -337,9 +345,8 @@
         spread(parts, send, recv, k, sems)
 
     absorb(0, wa, ka, senda, recva, 4, arcvd)
-    ring_r[NEIGHBOURS]()
+    ring_r[FAR]()
     ring_b[FORWARD]()
-    ring_r[FAR]()
     ring_r[FINISH]()
 
     projected = mm(qnat[...], wr[...].reshape(QR, 256))
@@ -347,8 +354,9 @@
     for h in range(HEADS):
         posq[h * 128 : h * 128 + 128, 0:DR] = projected[:, h * DR : h * DR + DR].astype(BF)
     spread([(posq, h * 128, slice(None)) for h in range(HEADS)], sendr, recvr, 8, rrcvd)
-    for step in ring_b[NEIGHBOURS:CLOSE]:
-        step()
+    ring_b[NEIGHBOURS]()
+    ring_b[FAR]()
+    ring_b[FINISH]()
     absorb(1, wb, kb, sendb, recvb, 5, brcvd)
 
     o = iota((64, 1), 0)

time: 67.5 us -> 65.3 us (0.967)
  Pallas kernels: 65.2 us -> 62.9 us
    pallas_call x1, Pallas kernels: 65.2 us -> 62.9 us  [body(): pl.pallas_call(kernel, out_shape=jax.ShapeDtypeStruct((STEPS, GROUPS, HEA...]
where the time goes in v4:
time: 65.3 us; the launch traced here: 65.1 us
  Pallas kernels  62.9 us (96%)
  local copies, waits for them, and re-layouts  1.57 us (2%)
  between operations  0.66 us (1%)
    pallas_call x1, Pallas kernels, body(): pl.pallas_call(kernel, out_shape=jax.ShapeDtypeStruct((STEPS, GROUPS, HEA...  62.9 us
    unnamed x1, local copies, waits for them, and re-layouts  1.57 us

profile of v4, /device:TPU:1, one launch (start us, length us, event | category | flops | bytes accessed | tf_op | source)
XLA Modules:
  0.0 65.1 jit_solution(2492040584265577236)
XLA Ops:
  0.7 62.9 %shard_map.91 = bf16[4,32,512]{2,1,0:T(8,128)(2,1)} custom-call(bf16[4,1536]{1,0:T(4,128)(2,1)} %bitcast.3, bf16[6,24576]{1,0:T(8,128)(2,1)} %wq_ref.1, bf16[2,16384]{1,0:T(2,128)(2,1)} %kw_ref.1, bf16[2,16384]{1,0:T(2,128)(2,1)} %vw_ref.1, bf16[1,2048,512]{2,1,0:T(8,128)(2,1)} %lat_hbm.1, bf16[1,64,2048]{2,1,0:T(8,128)(2,1)} %rope_hbm.1, ...), custom_call_target="tpu_custom_call" | custom-call | tf_op jit(solution)/shard_map/pallas_call | solution.py:459
  63.6 1.6 %copy.12 = bf16[4,32,512]{2,1,0:T(8,128)(2,1)} copy(bf16[4,32,512]{2,1,0:T(8,128)(2,1)} %shard_map.91) | data formatting | bytes 262144
